TPU v7x, 32 devices: a whole 2x2x4 slice. The times are simulated.
32 devices in a mesh: groups: 2 (over x), tile: 16 (over z, y, core).
Axes of the slice: x: 2, y: 2, z: 4, core: 2. Of those that a mesh axis runs over, the one named last changes fastest.
Arguments:
- source: bfloat16 [512, 2, 69, 128], P('tile', 'groups'), parts along dimension 1, may hold values from -42 to 42
- weights: bfloat16 [1536, 128, 128], P('tile'), may hold values from -0.5 to 0.5
- block_source: int32 [1536], P('tile'), may hold values from 0 to 31
- block_target: int32 [1536], P('tile'), may hold values from 0 to 511, as said below
- edge_flip: int32 [16, 2], P('tile'), may hold values 0 or 1
- norm_gain: float32 [69], replicated, may hold values from 0.1 to 1.9
- first_kernel: bfloat16 [9, 69, 69], replicated, may hold values from -0.25 to 0.25
- second_kernel: bfloat16 [9, 69, 69], replicated, may hold values from -0.25 to 0.25
Outputs:
- gridded: bfloat16 [512, 2, 69, 128], P('tile', 'groups'), parts along dimension 1
- smoothed: bfloat16 [512, 2, 69, 128], P('tile', 'groups'), parts along dimension 1
There are 2 independent parts, one for each index of `groups`. A program takes and returns all parts, laid end to end along the dimension named above; an argument that names none is the same for every part. Nothing has to cross between parts.
Inputs may be any that keep to these rules, and one draw needn't show every extreme that they name: `block_target`: band d lies at the latitude of tile position p = d mod 2, in column d // 2. Its entries name exactly 64 distinct target rows, all in tiles c * 2 + p or c * 2 + p + 1 (any column c, positions below 2). One band names at most 8 distinct rows of one tile, and every band at position 1 names exactly 8 rows of each tile at its own position.
All inputs are finite; a program needn't handle non-finite values. No bound on the sum of `edge_flip` on one device may be relied on, other than what follows from the above.
Results may differ from a plain program's by a relative error of at most 0.001.
The roundings to bfloat16 on the way count: a program that leaves them out, or rounds other values in their place, can miss the bound.
Values may be sent and summed in bfloat16 or wider, within the bound.
No kernel may reach another device: no remote copies, remote signals or barrier semaphores. Data moves between devices by JAX's collectives and lax.ppermute only.
A program may use at most 64 MiB of HBM per device.

v0:
```python
import functools

import jax
import jax.numpy as jnp
from jax import lax
from jax.experimental import pallas as pl
from jax.experimental.pallas import tpu as pltpu
from jax.sharding import PartitionSpec as P

BLOCK = 128
CHANNELS = 69
PADDED = 72
WIDE = 80
ROWS = 32
ROW_BITS = 5
HALF_ROWS = ROWS // 2
TILE_COLS = 8
CAP = 8
HALF = TILE_COLS // 2
GROUPS = 2 * TILE_COLS
COLUMN_ORDER = [half * HALF + at for at in range(HALF) for half in range(2)]
SLOTS = GROUPS * CAP
MARK = CHANNELS
BODY = 64
TAILS = (MARK + 1 - BODY) * CAP
MESSAGE = CAP * BODY + TAILS
CHUNK = 96
EPSILON = 1e-05
VMEM_LIMIT = 40 * 1024 * 1024
REGRID_VMEM = 60 * 1024 * 1024


def vmem():
    return pl.BlockSpec(memory_space=pltpu.VMEM)


def smem():
    return pl.BlockSpec(memory_space=pltpu.SMEM)


def split(value, size):
    if size & (size - 1) == 0:
        return value >> (size.bit_length() - 1), value & (size - 1)
    return lax.div(value, size), lax.rem(value, size)


def lanes(shape):
    return lax.broadcasted_iota(jnp.int32, shape, len(shape) - 1)


def regrid_kernel(
    column_rows, target_hbm, target_row_hbm, index_hbm, source_hbm, weight_hbm, *rest
):
    same_out, next_outs = rest[0], rest[1 : 1 + TILE_COLS]
    (
        target_ref,
        target_row_ref,
        index_ref,
        source,
        weight,
        wide,
        field,
        sums,
        message,
        tails,
        plan,
        plan_scalars,
        plan_sem,
        in_sems,
        weight_sems,
        out_sems,
    ) = rest[1 + TILE_COLS :]
    entries = weight.shape[0]
    chunks = entries // CHUNK
    tile = lax.axis_index("tile")
    column, position = split(tile, column_rows)

    small_copies = [
        pltpu.make_async_copy(target_row_hbm, target_row_ref, in_sems.at[0]),
        pltpu.make_async_copy(target_hbm, target_ref, in_sems.at[1]),
        pltpu.make_async_copy(index_hbm, index_ref, in_sems.at[2]),
    ]
    source_copy = pltpu.make_async_copy(source_hbm, source, in_sems.at[3])
    for copy in small_copies:
        copy.start()
    source_copy.start()

    def chunk_copy(chunk):
        part = pl.ds(chunk * CHUNK, CHUNK)
        return pltpu.make_async_copy(weight_hbm.at[part], weight.at[part], weight_sems.at[chunk])

    for chunk in range(chunks):
        chunk_copy(chunk).start()

    small_copies[0].wait()
    target = target_row_ref[...]
    owner, row = split(target, ROWS)
    owner_column, owner_position = split(owner, column_rows)
    place = ((owner_column & (HALF - 1)) << 1) + (owner_column >= HALF).astype(jnp.int32)
    group = jnp.where(owner_position == position, place, TILE_COLS + (owner_column ^ column))
    key = group * ROWS + row
    square = (entries, entries)
    down = lax.broadcasted_iota(jnp.int32, square, 0)
    along = lanes(square)
    key_along = jnp.broadcast_to(key.astype(jnp.float32), square)
    key_down = jnp.broadcast_to(
        jnp.sum(jnp.where(down == along, key_along, 0.0), axis=1, keepdims=True), square
    )
    equal = key_along == key_down
    doubles = jnp.sum(jnp.where(equal & (along < down), 1.0, 0.0), axis=1, keepdims=True)
    in_group = (key_down.astype(jnp.int32) >> ROW_BITS) == (key_along.astype(jnp.int32) >> ROW_BITS)
    below = in_group & (key_down < key_along) & (jnp.broadcast_to(doubles, square) == 0.0)
    rank = jnp.sum(jnp.where(below, 1.0, 0.0), axis=0, keepdims=True)
    mentions = jnp.sum(jnp.where(equal & (down < along), 1.0, 0.0), axis=0, keepdims=True)
    slots = group * CAP + rank.astype(jnp.int32)
    plan[...] = slots + jnp.where(mentions == 0.0, SLOTS, 0)
    plan_copy = pltpu.make_async_copy(plan, plan_scalars, plan_sem)
    plan_copy.start()

    for slot in range(SLOTS):
        tails[pl.ds(slot * 8, 8), :] = jnp.full((8, BLOCK), ROWS, jnp.float32)
    wide[pl.ds(CHANNELS * ROWS, (PADDED - CHANNELS) * ROWS), :] = jnp.zeros(
        ((PADDED - CHANNELS) * ROWS, BLOCK), jnp.float32
    )
    nothing = jnp.zeros((WIDE - PADDED, BLOCK), jnp.float32)
    source_copy.wait()
    wide[pl.ds(0, CHANNELS * ROWS), :] = source[...].astype(jnp.float32)
    turned = jnp.transpose(wide[...].reshape(PADDED, ROWS, BLOCK), (1, 0, 2))
    for row in range(ROWS):
        field[row] = jnp.concatenate([turned[row], nothing], axis=0).astype(jnp.bfloat16)
    is_mark = lax.broadcasted_iota(jnp.int32, (8, BLOCK), 0) == MARK - BODY
    blank = jnp.zeros((WIDE, BLOCK), jnp.bfloat16)
    small_copies[1].wait()
    small_copies[2].wait()
    plan_copy.wait()

    for chunk in range(chunks):
        chunk_copy(chunk).wait()
        for entry in range(chunk * CHUNK, (chunk + 1) * CHUNK, 2):
            one = jnp.concatenate([field[index_ref[entry]], blank], axis=1)
            two = jnp.concatenate([blank, field[index_ref[entry + 1]]], axis=1)
            products = jnp.dot(
                jnp.concatenate([one, two], axis=0),
                weight[entry : entry + 2].reshape(2 * BLOCK, BLOCK),
                preferred_element_type=jnp.float32,
            )
            for at in range(2):
                code = plan_scalars[0, entry + at]
                slot = code & (SLOTS - 1)
                row = split(target_ref[entry + at], ROWS)[1]
                product = products[at * WIDE : at * WIDE + PADDED]
                total = jnp.where(code >= SLOTS, 0.0, sums[slot]) + product
                sums[slot] = total
                group, place = split(slot, CAP)
                message[group, pl.ds(pl.multiple_of(place * BODY, BODY), BODY), :] = total[
                    :BODY
                ].astype(jnp.bfloat16)
                tails[pl.ds(pl.multiple_of(slot * 8, 8), 8), :] = jnp.where(
                    is_mark, row.astype(jnp.float32), total[BODY:]
                )
    copies = []
    for group in range(GROUPS):
        start = group * CAP * 8
        ends = [tails[pl.ds(start + at, CAP, stride=8), :] for at in range(MARK + 1 - BODY)]
        message[group, CAP * BODY :] = jnp.concatenate(ends, axis=0).astype(jnp.bfloat16)
        if group < TILE_COLS:
            out = same_out.at[pl.ds(group * MESSAGE, MESSAGE)]
        else:
            out = next_outs[group - TILE_COLS]
        copies.append(pltpu.make_async_copy(message.at[group], out, out_sems.at[group]))
        copies[-1].start()
    for copy in copies:
        copy.wait()


def regrid(target, source_index, field, weights, column_rows):
    piece = jax.ShapeDtypeStruct((MESSAGE, BLOCK), jnp.bfloat16)
    same = jax.ShapeDtypeStruct((TILE_COLS * MESSAGE, BLOCK), jnp.bfloat16)
    hbm = pl.BlockSpec(memory_space=pl.ANY)
    entries = weights.shape[0]
    return pl.pallas_call(
        functools.partial(regrid_kernel, column_rows),
        in_specs=[hbm] * 5,
        out_specs=[hbm] * (1 + TILE_COLS),
        out_shape=[same] + [piece] * TILE_COLS,
        scratch_shapes=[
            pltpu.SMEM(target.shape, jnp.int32),
            pltpu.VMEM((1, entries), jnp.int32),
            pltpu.SMEM(source_index.shape, jnp.int32),
            pltpu.VMEM(field.shape, jnp.bfloat16),
            pltpu.VMEM(weights.shape, jnp.bfloat16),
            pltpu.VMEM((PADDED * ROWS, BLOCK), jnp.float32),
            pltpu.VMEM((ROWS, WIDE, BLOCK), jnp.bfloat16),
            pltpu.VMEM((SLOTS, PADDED, BLOCK), jnp.float32),
            pltpu.VMEM((GROUPS, MESSAGE, BLOCK), jnp.bfloat16),
            pltpu.VMEM((SLOTS * 8, BLOCK), jnp.float32),
            pltpu.VMEM((1, entries), jnp.int32),
            pltpu.SMEM((1, entries), jnp.int32),
            pltpu.SemaphoreType.DMA,
            pltpu.SemaphoreType.DMA((4,)),
            pltpu.SemaphoreType.DMA((entries // CHUNK,)),
            pltpu.SemaphoreType.DMA((GROUPS,)),
        ],
        compiler_params=pltpu.CompilerParams(vmem_limit_bytes=REGRID_VMEM),
        name="regrid",
    )(target, target.reshape(1, -1), source_index, field, weights)


def normalized(rounded, gain):
    value = rounded.astype(jnp.float32)
    real = lax.broadcasted_iota(jnp.int32, (PADDED - BODY, BLOCK), 0) < CHANNELS - BODY
    value = jnp.concatenate([value[:BODY], jnp.where(real, value[BODY:], 0.0)], axis=0)
    square = jnp.sum(value * value, axis=0, keepdims=True) * (1.0 / CHANNELS)
    scaled = value * lax.rsqrt(square + EPSILON) * gain
    nothing = jnp.zeros((WIDE - PADDED, BLOCK), jnp.float32)
    return jnp.concatenate([scaled, nothing], axis=0).astype(jnp.bfloat16)


def gather_kernel(column_rows, flip_ref, gain_ref, same, *rest):
    nexts = rest[:TILE_COLS]
    summed, upward, downward, strip_out, tails = rest[TILE_COLS:]
    position = lax.rem(lax.axis_index("tile"), column_rows)
    summed[...] = jnp.zeros_like(summed)

    def add(group, piece):
        ends = piece[CAP * BODY :].astype(jnp.float32)
        tails[group, :TAILS] = ends
        rows = ends[TAILS - CAP :].astype(jnp.int32)
        for place in range(CAP):
            row = rows[place, 0]
            body = piece[place * BODY : (place + 1) * BODY].astype(jnp.float32)
            summed[row, :BODY] = summed[row, :BODY] + body
            tail = tails[group, pl.ds(place, 8, stride=CAP), :]
            summed[row, BODY:] = summed[row, BODY:] + tail

    tails[:, TAILS:] = jnp.zeros((GROUPS, 8 * CAP - TAILS, BLOCK), jnp.float32)
    for group in range(TILE_COLS):
        add(group, same.at[pl.ds(group * MESSAGE, MESSAGE)])

    @pl.when(position > 0)
    def _():
        for group in range(TILE_COLS):
            add(TILE_COLS + group, nexts[group])

    gain = gain_ref[...]
    for at in range(2):
        upward[at] = normalized(summed[at].astype(jnp.bfloat16), gain)
        downward[at] = normalized(summed[ROWS - 2 + at].astype(jnp.bfloat16), gain)
    lane = lanes((PADDED, BLOCK))
    strip = jnp.zeros((PADDED, BLOCK), jnp.bfloat16)
    for row in range(ROWS):
        rounded = summed[row].astype(jnp.bfloat16)
        strip = jnp.where((lane >> 2) == row, pltpu.roll(rounded, 4 * row + 2, 1), strip)
    to_lane = lanes((BLOCK, BLOCK))
    from_lane = 4 * (to_lane & (ROWS - 1)) + (((to_lane >> ROW_BITS) + 2) & 3)
    order = lax.broadcasted_iota(jnp.int32, (BLOCK, BLOCK), 0) == from_lane
    strip = jnp.dot(
        normalized(strip, gain), order.astype(jnp.bfloat16), preferred_element_type=jnp.float32
    )
    channel = lax.broadcasted_iota(jnp.int32, (WIDE, BLOCK), 0)
    for side in range(2):
        strip = jnp.where(channel == CHANNELS + side, flip_ref[0, side].astype(jnp.float32), strip)
    strip = strip.astype(jnp.bfloat16)
    upward[2] = strip
    downward[2] = strip
    strip_out[...] = strip


def normalize_kernel(gain_ref, summed, gridded, normed):
    gain = gain_ref[...]
    for row in range(ROWS):
        rounded = summed[row].astype(jnp.bfloat16)
        gridded[row] = rounded
        normed[row] = normalized(rounded, gain)


def normalize_rows(gain, summed):
    return pl.pallas_call(
        normalize_kernel,
        in_specs=[vmem()] * 2,
        out_specs=[vmem()] * 2,
        out_shape=[GRIDDED, FIELD],
        compiler_params=pltpu.CompilerParams(vmem_limit_bytes=VMEM_LIMIT),
        cost_estimate=pl.CostEstimate(
            flops=10 * ROWS * PADDED * BLOCK, bytes_accessed=2 << 20, transcendentals=0
        ),
        name="normalize_rows",
    )(gain, summed)


SUMMED = jax.ShapeDtypeStruct((ROWS + 1, PADDED, BLOCK), jnp.float32)
GRIDDED = jax.ShapeDtypeStruct((ROWS, PADDED, BLOCK), jnp.bfloat16)
FIELD = jax.ShapeDtypeStruct((ROWS, WIDE, BLOCK), jnp.bfloat16)
RIM = jax.ShapeDtypeStruct((3, WIDE, BLOCK), jnp.bfloat16)
STRIP_COLUMNS = (0, 1, BLOCK - 2, BLOCK - 1)
STRIP = jax.ShapeDtypeStruct((WIDE, BLOCK), jnp.bfloat16)


def gather_rows(column_rows, edge_flip, gain, same, nexts):
    return pl.pallas_call(
        functools.partial(gather_kernel, column_rows),
        in_specs=[smem()] + [vmem()] * (2 + TILE_COLS),
        out_specs=[vmem()] * 4,
        out_shape=[SUMMED, RIM, RIM, STRIP],
        scratch_shapes=[pltpu.VMEM((GROUPS, 8 * CAP, BLOCK), jnp.float32)],
        compiler_params=pltpu.CompilerParams(vmem_limit_bytes=VMEM_LIMIT),
        name="gather_rows",
    )(edge_flip, gain, same, *nexts)


def turn_kernel(field, out):
    turned = jnp.transpose(field[...].astype(jnp.float32), (1, 0, 2))
    out[...] = turned[:CHANNELS].reshape(CHANNELS * ROWS, BLOCK).astype(jnp.bfloat16)


def channels_first(field):
    return pl.pallas_call(
        turn_kernel,
        in_specs=[vmem()],
        out_specs=vmem(),
        out_shape=jax.ShapeDtypeStruct((CHANNELS * ROWS, BLOCK), jnp.bfloat16),
        compiler_params=pltpu.CompilerParams(vmem_limit_bytes=VMEM_LIMIT),
        name="channels_first",
    )(field)


def shifted_columns(value, left_end, right_end):
    lane = lanes((WIDE, BLOCK))
    left = jnp.where(lane == 0, left_end, pltpu.roll(value, 1, 1))
    right = jnp.where(lane == BLOCK - 1, right_end, pltpu.roll(value, BLOCK - 1, 1))
    return jnp.concatenate([left, value, right], axis=0)


def tap_sums(taps, one, two):
    both = jnp.concatenate([one, two], axis=1)
    result = jnp.dot(taps, both, preferred_element_type=jnp.float32)
    return result[:, :BLOCK], result[:, BLOCK:]


def row_tap(sums, at):
    return sums[at * WIDE : (at + 1) * WIDE]


def activated(value):
    return jax.nn.gelu(value).astype(jnp.bfloat16)


def inner_kernel(taps_ref, field, hidden, ends, sides, partial):
    taps = taps_ref[...]
    blank = jnp.zeros((WIDE, BLOCK), jnp.bfloat16)
    for row in range(0, ROWS, 2):
        partial[row], partial[row + 1] = tap_sums(
            taps,
            shifted_columns(field[row], blank, blank),
            shifted_columns(field[row + 1], blank, blank),
        )
    lane = lanes((WIDE, BLOCK))
    west = jnp.zeros((WIDE, BLOCK), jnp.float32)
    east = jnp.zeros((WIDE, BLOCK), jnp.float32)
    for row in range(ROWS):
        value = partial[row, WIDE : 2 * WIDE]
        if row > 0:
            value = value + partial[row - 1, :WIDE]
        if row < ROWS - 1:
            value = value + partial[row + 1, 2 * WIDE :]
        if row == 0:
            ends[0] = value
        elif row == ROWS - 1:
            ends[1] = value
        else:
            hidden[row] = jnp.where((lane == 0) | (lane == BLOCK - 1), blank, activated(value))
        west = jnp.where(lane == row, pltpu.roll(value, row, 1), west)
        east = jnp.where(lane == row, pltpu.roll(value, row + 1, 1), east)
    hidden[0] = blank
    hidden[ROWS - 1] = blank
    sides[0] = west
    sides[1] = east


def inner_convolution(taps, field):
    pair = jax.ShapeDtypeStruct((2, WIDE, BLOCK), jnp.float32)
    return pl.pallas_call(
        inner_kernel,
        in_specs=[vmem()] * 2,
        out_specs=[vmem()] * 3,
        out_shape=[FIELD, pair, pair],
        scratch_shapes=[pltpu.VMEM((ROWS, 3 * WIDE, BLOCK), jnp.float32)],
        compiler_params=pltpu.CompilerParams(vmem_limit_bytes=VMEM_LIMIT),
        cost_estimate=pl.CostEstimate(
            flops=2 * 9 * WIDE * WIDE * ROWS * BLOCK, bytes_accessed=2 << 20, transcendentals=0
        ),
        name="inner_convolution",
    )(taps, field)


def second_kernel_inner(taps_ref, hidden, gridded, base, partial):
    taps = taps_ref[...]
    blank = jnp.zeros((WIDE, BLOCK), jnp.bfloat16)
    for row in range(0, ROWS, 2):
        partial[row], partial[row + 1] = tap_sums(
            taps,
            shifted_columns(hidden[row], blank, blank),
            shifted_columns(hidden[row + 1], blank, blank),
        )
    for row in range(ROWS):
        value = gridded[row].astype(jnp.float32) + partial[row, WIDE : WIDE + PADDED]
        if row > 0:
            value = value + partial[row - 1, :PADDED]
        if row < ROWS - 1:
            value = value + partial[row + 1, 2 * WIDE : 2 * WIDE + PADDED]
        base[row] = value


def inner_second_convolution(taps, hidden, gridded):
    return pl.pallas_call(
        second_kernel_inner,
        in_specs=[vmem()] * 3,
        out_specs=vmem(),
        out_shape=jax.ShapeDtypeStruct((ROWS, PADDED, BLOCK), jnp.float32),
        scratch_shapes=[pltpu.VMEM((ROWS, 3 * WIDE, BLOCK), jnp.float32)],
        compiler_params=pltpu.CompilerParams(vmem_limit_bytes=VMEM_LIMIT),
        cost_estimate=pl.CostEstimate(
            flops=2 * 9 * WIDE * WIDE * ROWS * BLOCK, bytes_accessed=2 << 20, transcendentals=0
        ),
        name="inner_second_convolution",
    )(taps, hidden, gridded)


def pack_kernel(above, below, own, to_west, to_east):
    low = lanes((WIDE, BLOCK)) < BLOCK // 2
    before, strip, after = above[2], own[...], below[2]

    def other_half(plane):
        return pltpu.roll(plane, BLOCK // 2, 1)

    outer = jnp.where(low, after, before)
    to_east[0] = jnp.where(low, other_half(strip), after)
    to_east[1] = outer
    to_west[0] = jnp.where(low, strip, other_half(before))
    to_west[1] = outer


def half_strip_packs(above, below, own):
    pack = jax.ShapeDtypeStruct((2, WIDE, BLOCK), jnp.bfloat16)
    return pl.pallas_call(
        pack_kernel,
        in_specs=[vmem()] * 3,
        out_specs=[vmem()] * 2,
        out_shape=[pack, pack],
        compiler_params=pltpu.CompilerParams(vmem_limit_bytes=VMEM_LIMIT),
        name="half_strip_packs",
    )(above, below, own)


def half_strips(west_pack, east_pack):
    low = lanes((WIDE, BLOCK)) < BLOCK // 2

    def other_half(plane):
        return pltpu.roll(plane, BLOCK // 2, 1)

    def both_halves(plane):
        return jnp.where(low, plane, other_half(plane))

    return {
        -4: west_pack[1],
        -3: both_halves(west_pack[0]),
        -2: jnp.where(low, west_pack[1], west_pack[0]),
        2: jnp.where(low, other_half(east_pack[0]), east_pack[1]),
        3: both_halves(east_pack[0]),
        4: east_pack[1],
    }


def strip_plan(column_rows):
    if column_rows == 2:
        return [], 3, 1
    return [-2, 2], column_rows, 2


def conv_kernel(
    column_rows,
    first_taps_ref,
    second_taps_ref,
    field,
    base,
    ends_ref,
    sides_ref,
    above,
    below,
    own_strip,
    *rest,
):
    near, far, reach = strip_plan(column_rows)
    near_strips, (west_pack, east_pack) = rest[: len(near)], rest[len(near) : len(near) + 2]
    smoothed, unturned, halves, sems = rest[len(near) + 2 :]
    count = lax.axis_size("tile")
    tile = lax.axis_index("tile")
    lane = lanes((WIDE, BLOCK))
    last = ROWS + 1
    R = column_rows
    blank = jnp.zeros((WIDE, BLOCK), jnp.bfloat16)

    strips = {-1: above[2], 0: own_strip[...], 1: below[2]}
    strips.update((shift, ref[...]) for shift, ref in zip(near, near_strips))
    if R == 2:
        strips.update(half_strips(west_pack, east_pack))
    else:
        for at in range(-reach, reach + 1):
            strips[at - far], strips[at + far] = west_pack[at + reach], east_pack[at + reach]

    def place(shift):
        return lax.rem(tile + shift + count, count)

    def ends(shift, before, after, middle):
        before = jnp.where(place(shift) > 0, before, blank)
        after = jnp.where(place(shift) < count - 1, after, blank)
        return jnp.where(lane == 0, before, jnp.where(lane == last, after, middle))

    memo = {}

    def padded_column(shift, which):
        if (shift, which) not in memo:
            base = which * ROWS
            memo[shift, which] = ends(
                shift,
                pltpu.roll(strips[shift - 1], (1 - base - ROWS) % BLOCK, 1),
                pltpu.roll(strips[shift + 1], (last - base) % BLOCK, 1),
                pltpu.roll(strips[shift], (1 - base) % BLOCK, 1),
            )
        return memo[shift, which]

    row_id = lax.broadcasted_iota(jnp.int32, (BLOCK, BLOCK), 0)
    reversal = (row_id + lanes((BLOCK, BLOCK)) == last).astype(jnp.bfloat16)

    def reversed_lanes(planes):
        stacked = jnp.concatenate(planes, axis=0)
        turned_round = jnp.dot(stacked, reversal, preferred_element_type=jnp.float32)
        return [row_tap(turned_round, at) for at in range(len(planes))]

    def choose(shift, which, turned_round, plain):
        flips = strips[shift].astype(jnp.float32)[CHANNELS + which : CHANNELS + which + 1]
        return jnp.where(flips > 0.5, turned_round, plain.astype(jnp.float32)).astype(jnp.bfloat16)

    west_of = {shift: (shift - R, 3) for shift in {-1, 0, 1, R - 1, R, R + 1}}
    east_of = {shift: (shift + R, 0) for shift in {-1, 0, 1, -R - 1, -R, -R + 1}}
    keys = sorted(set(west_of.values()) | set(east_of.values()))
    flipped = dict(zip(keys, reversed_lanes([padded_column(*key) for key in keys])))
    west = {
        shift: choose(shift, 0, flipped[west_of[shift]], padded_column(*west_of[shift]))
        for shift in sorted(west_of)
    }
    east = {
        shift: choose(shift, 1, flipped[east_of[shift]], padded_column(*east_of[shift]))
        for shift in sorted(east_of)
    }

    def columns(value, west_plane, west_row, east_plane, east_row):
        return shifted_columns(
            value,
            pltpu.roll(west_plane, (BLOCK - west_row) % BLOCK, 1),
            pltpu.roll(east_plane, BLOCK - 1 - east_row, 1),
        )

    def along(result):
        return (
            row_tap(result, 0)
            + pltpu.roll(row_tap(result, 1), BLOCK - 1, 1)
            + pltpu.roll(row_tap(result, 2), BLOCK - 2, 1)
        )

    first_taps = first_taps_ref[...]
    up = [jnp.where(tile > 0, above[at], blank) for at in range(2)]
    down = [jnp.where(tile < count - 1, below[at], blank) for at in range(2)]
    from_up, from_down = tap_sums(
        first_taps, shifted_columns(up[1], blank, blank), shifted_columns(down[0], blank, blank)
    )
    from_up, from_down = row_tap(from_up, 0), row_tap(from_down, 2)
    from_west, from_east = tap_sums(
        first_taps,
        jnp.concatenate([west[0], blank, blank], axis=0),
        jnp.concatenate([blank, blank, east[0]], axis=0),
    )
    from_west, from_east = along(from_west), along(from_east)
    first = ends_ref[0] + from_up
    first = first + jnp.where(lane == 0, from_west, 0.0)
    first = first + jnp.where(lane == BLOCK - 1, pltpu.roll(from_east, BLOCK - 1, 1), 0.0)
    final = ends_ref[1] + from_down
    final = final + jnp.where(lane == 0, pltpu.roll(from_west, BLOCK - ROWS + 1, 1), 0.0)
    final = final + jnp.where(lane == BLOCK - 1, pltpu.roll(from_east, BLOCK - ROWS, 1), 0.0)
    first, final = activated(first), activated(final)
    first_column = activated(sides_ref[0] + from_west)
    last_column = activated(sides_ref[1] + from_east)

    upper = jnp.zeros((WIDE, BLOCK), jnp.float32)
    lower = jnp.zeros((WIDE, BLOCK), jnp.float32)
    for at, (high, low) in enumerate(
        [(up[0], field[ROWS - 1]), (up[1], down[0]), (field[0], down[1])]
    ):
        from_row = ROWS - 1 + at
        one, two = tap_sums(
            row_tap(first_taps, at),
            columns(high, west[-1], from_row, east[-1], from_row),
            columns(low, west[1], at, east[1], at),
        )
        upper += one
        lower += two
    top = jnp.where(tile > 0, activated(upper), blank)
    bottom = jnp.where(tile < count - 1, activated(lower), blank)

    west_hidden, east_hidden = {}, {}
    for at in (-1, 0, 1):
        q = at - R
        one = jnp.concatenate([padded_column(q, 2), padded_column(q, 3), east[q]], axis=0)
        q = at + R
        two = jnp.concatenate([west[q], padded_column(q, 0), padded_column(q, 1)], axis=0)
        one, two = tap_sums(first_taps, one, two)
        west_hidden[at], east_hidden[at] = activated(along(one)), activated(along(two))

    def hidden_side(shift, values):
        return ends(
            shift,
            pltpu.roll(values[-1], BLOCK - ROWS + 1, 1),
            pltpu.roll(values[1], last, 1),
            pltpu.roll(values[0], 1, 1),
        )

    plain = [hidden_side(-R, west_hidden), hidden_side(R, east_hidden)]
    west_side, east_side = [
        choose(0, which, turned_side, plain[which])
        for which, turned_side in enumerate(reversed_lanes(plain))
    ]

    second_taps = second_taps_ref[...]
    from_top, from_first = tap_sums(
        second_taps,
        columns(top, west_side, 0, east_side, 0),
        columns(first, west_side, 1, east_side, 1),
    )
    from_final, from_bottom = tap_sums(
        second_taps,
        columns(final, west_side, ROWS, east_side, ROWS),
        columns(bottom, west_side, last, east_side, last),
    )
    rim_rows = {
        0: row_tap(from_top, 0) + row_tap(from_first, 1),
        1: row_tap(from_first, 0),
        ROWS - 2: row_tap(from_final, 2),
        ROWS - 1: row_tap(from_final, 1) + row_tap(from_bottom, 2),
    }

    other = (lane >= 2) & (lane < ROWS)

    def other_rows(plane):
        return jnp.where(other, plane, blank)

    near_west, near_east = other_rows(west_side), other_rows(east_side)
    first_column = other_rows(pltpu.roll(first_column, 1, 1))
    last_column = other_rows(pltpu.roll(last_column, 1, 1))
    to_0, to_1 = tap_sums(
        second_taps,
        jnp.concatenate([near_west, first_column, blank], axis=0),
        jnp.concatenate([first_column, blank, blank], axis=0),
    )
    to_127, to_126 = tap_sums(
        second_taps,
        jnp.concatenate([blank, last_column, near_east], axis=0),
        jnp.concatenate([blank, blank, last_column], axis=0),
    )
    parts, to_lanes = [], []
    for at, sums in enumerate((to_126, to_127, to_0, to_1)):
        sums = along(sums)
        high = sums.astype(jnp.bfloat16)
        sums = sums - high.astype(jnp.float32)
        middle = sums.astype(jnp.bfloat16)
        low = (sums - middle.astype(jnp.float32)).astype(jnp.bfloat16)
        parts.append(jnp.concatenate([high, middle, low], axis=0))
        to_lanes.append((lanes((BLOCK, BLOCK)) == 4 * row_id + at).astype(jnp.bfloat16))
    spread = jnp.dot(
        jnp.concatenate(parts, axis=1),
        jnp.concatenate(to_lanes, axis=0),
        preferred_element_type=jnp.float32,
    )
    spread = row_tap(spread, 0) + (row_tap(spread, 1) + row_tap(spread, 2))

    rim_lanes = lanes((PADDED, BLOCK))
    rim_lanes = (rim_lanes < 2) | (rim_lanes >= BLOCK - 2)
    spread = spread[:PADDED]
    copies = []
    for half in range(2):
        for row in range(half * HALF_ROWS, (half + 1) * HALF_ROWS):
            value = base[row] + jnp.where(
                rim_lanes, pltpu.roll(spread, (BLOCK - 4 * row - 2) % BLOCK, 1), 0.0
            )
            if row in rim_rows:
                value = value + rim_rows[row][:PADDED]
            unturned[half, row - half * HALF_ROWS] = value
        halves[half] = jnp.transpose(unturned[half], (1, 0, 2))[:CHANNELS].astype(jnp.bfloat16)
        rows = pl.ds(half * HALF_ROWS, HALF_ROWS)
        copies.append(pltpu.make_async_copy(halves.at[half], smoothed.at[:, rows], sems.at[half]))
        copies[-1].start()
    for copy in copies:
        copy.wait()


def convolutions(column_rows, *operands):
    return pl.pallas_call(
        functools.partial(conv_kernel, column_rows),
        in_specs=[vmem()] * len(operands),
        out_specs=pl.BlockSpec(memory_space=pl.ANY),
        out_shape=jax.ShapeDtypeStruct((CHANNELS, ROWS, BLOCK), jnp.bfloat16),
        scratch_shapes=[
            pltpu.VMEM((2, HALF_ROWS, PADDED, BLOCK), jnp.float32),
            pltpu.VMEM((2, CHANNELS, HALF_ROWS, BLOCK), jnp.bfloat16),
            pltpu.SemaphoreType.DMA((2,)),
        ],
        compiler_params=pltpu.CompilerParams(vmem_limit_bytes=VMEM_LIMIT),
        name="convolutions",
    )(*operands)


def tap_matrix(kernel):
    pad = WIDE - CHANNELS
    taps = jnp.pad(kernel, ((0, 0), (0, pad), (0, pad))).reshape(3, 3, WIDE, WIDE)
    return taps.transpose(0, 2, 1, 3).reshape(3 * WIDE, 3 * WIDE)


def from_shift(value, shift):
    count = lax.axis_size("tile")
    return lax.ppermute(value, "tile", [(i, (i - shift) % count) for i in range(count)])


def per_device(
    source, weights, block_source, block_target, edge_flip, norm_gain, first_kernel, second_kernel
):
    count = lax.axis_size("tile")
    column_rows = count // TILE_COLS
    field = source.reshape(ROWS, CHANNELS, BLOCK).transpose(1, 0, 2).reshape(-1, BLOCK)
    same, *nexts = regrid(block_target, block_source, field, weights, column_rows)

    for across in range(TILE_COLS):
        pairs = [
            (c * column_rows + p, (c ^ across) * column_rows + p + 1)
            for c in range(TILE_COLS)
            for p in range(column_rows - 1)
        ]
        nexts[across] = lax.ppermute(nexts[across], "tile", pairs)
    nexts = [nexts[across] for across in (0, 1, 2, 4, 7, 5, 6, 3)]
    same = lax.all_to_all(
        same,
        "tile",
        0,
        0,
        axis_index_groups=[
            [c * column_rows + p for c in COLUMN_ORDER] for p in range(column_rows)
        ],
        tiled=True,
    )

    gain = jnp.broadcast_to(
        jnp.pad(norm_gain, (0, PADDED - CHANNELS))[:, None], (PADDED, BLOCK)
    )
    first_taps, second_taps = tap_matrix(first_kernel), tap_matrix(second_kernel)
    same, nexts, gain, first_taps, second_taps = lax.optimization_barrier(
        (same, nexts, gain, first_taps, second_taps)
    )
    summed, upward, downward, strip = gather_rows(column_rows, edge_flip, gain, same, nexts)
    rims = [from_shift(downward, -1), from_shift(upward, 1)]
    near, far, reach = strip_plan(column_rows)
    strips = [from_shift(strip, shift) for shift in near]
    gridded, normed = normalize_rows(gain, summed)
    inner = inner_convolution(first_taps, normed)
    if column_rows == 2:
        to_west, to_east = half_strip_packs(*rims, strip)
    else:
        held = {-1: rims[0][2], 0: strip, 1: rims[1][2], **dict(zip(near, strips))}
        to_west = to_east = jnp.stack([held[at] for at in range(-reach, reach + 1)])
    to_west, to_east, inner = lax.optimization_barrier((to_west, to_east, inner))
    strips += [from_shift(to_east, -far), from_shift(to_west, far)]
    gridded_out = channels_first(gridded)
    hidden, *unfinished = inner
    base = inner_second_convolution(second_taps, hidden, gridded)
    smoothed = convolutions(
        column_rows, first_taps, second_taps, normed, base, *unfinished, *rims, strip, *strips
    )

    def placed(value):
        return value.reshape(CHANNELS, ROWS, BLOCK).transpose(1, 0, 2)[:, None]

    return placed(gridded_out), placed(smoothed)


def solution(mesh):
    in_specs = (
        P("tile", "groups", None, None),
        P("tile", None, None),
        P("tile"),
        P("tile"),
        P("tile", None),
        P(),
        P(),
        P(),
    )
    out_specs = (P("tile", "groups", None, None), P("tile", "groups", None, None))
    return jax.shard_map(
        per_device, mesh=mesh, in_specs=in_specs, out_specs=out_specs, check_vma=False
    )
```

profile of v0, /device:TPU:1, one launch (start us, length us, event | category | flops | bytes accessed | tf_op | source)
XLA Modules:
  0.0 67.1 jit_solution(17727017672554984758)
XLA Ops:
  0.6 5.0 %regrid.1 = (bf16[4480,128]{1,0:T(8,128)(2,1)}, bf16[560,128]{1,0:T(8,128)(2,1)}, bf16[560,128]{1,0:T(8,128)(2,1)}, bf16[560,128]{1,0:T(8,128)(2,1)}, bf16[560,1...) custom-call(s32[96]{0:T(128)} %target_hbm.1, ...), custom_call_target="tpu_custom_call" | custom-call | tf_op jit(solution)/shard_map/regrid/pallas_call | solution.py:181
  5.6 0.0 copy-start.9
  5.6 0.0 copy-start.8
  5.7 0.0 copy-start.1
  5.7 0.0 copy-start.2
  5.7 6.5 %all-to-all-start = ((bf16[8,560,128]{2,1,0:T(8,128)(2,1)}), bf16[8,560,128]{2,1,0:T(8,128)(2,1)S(1)}, u32[]{:S(2)}, u32[]{:S(2)}) async-start(bf16[8,560,128]{2,1,0:T(8,128)(2,1)} %bitcast.25), calls=%async_computation | async-start | bytes 2293760 | tf_op jit(solution)/shard_map/all_to_all | solution.py:748
  12.3 1.3 %collective-permute-start = (bf16[560,128]{1,0:T(8,128)(2,1)S(1)}, bf16[560,128]{1,0:T(8,128)(2,1)S(1)}, u32[]{:S(2)}, u32[]{:S(2)}) collective-permute-start(bf16[560,128]{1,0:T(8,128)(2,1)S(1)} %copy-done.9), channel_id=1, source_target_pairs={{0,1},{2,3},{4,5},{6,7},{8,9},{10,11},{12,13},{14,15},{16,17},{18,... | collective-permute-start | bytes 430088 | tf_op jit(solution)/shard_map/ppermute | solution.py:746
  13.6 0.0 copy-start
  13.6 1.3 %collective-permute-start.1 = (bf16[560,128]{1,0:T(8,128)(2,1)S(1)}, bf16[560,128]{1,0:T(8,128)(2,1)S(1)}, u32[]{:S(2)}, u32[]{:S(2)}) collective-permute-start(bf16[560,128]{1,0:T(8,128)(2,1)S(1)} %copy-done.8), channel_id=1, source_target_pairs={{0,3},{2,1},{4,7},{6,5},{8,11},{10,9},{12,15},{14,13},{16,19},{18,... | collective-permute-start | bytes 430088 | tf_op jit(solution)/shard_map/ppermute | solution.py:746
  14.9 0.0 copy-done.7
  14.9 1.3 %collective-permute-start.2 = (bf16[560,128]{1,0:T(8,128)(2,1)S(1)}, bf16[560,128]{1,0:T(8,128)(2,1)S(1)}, u32[]{:S(2)}, u32[]{:S(2)}) collective-permute-start(bf16[560,128]{1,0:T(8,128)(2,1)S(1)} %copy-done.7), channel_id=1, source_target_pairs={{0,5},{2,7},{4,1},{6,3},{8,13},{10,15},{12,9},{14,11},{16,21},{18,... | collective-permute-start | bytes 430088 | tf_op jit(solution)/shard_map/ppermute | solution.py:746
  16.2 1.3 %collective-permute-start.3 = (bf16[560,128]{1,0:T(8,128)(2,1)}, bf16[560,128]{1,0:T(8,128)(2,1)S(1)}, u32[]{:S(2)}, u32[]{:S(2)}) collective-permute-start(bf16[560,128]{1,0:T(8,128)(2,1)} %get-tuple-element.43), channel_id=1, source_target_pairs={{0,9},{2,11},{4,13},{6,15},{8,1},{10,3},{12,5},{14,7},{16,25},{18,... | collective-permute-start | bytes 430088 | tf_op jit(solution)/shard_map/ppermute | solution.py:746
  17.5 0.0 copy-done.6
  17.5 1.3 %collective-permute-start.4 = (bf16[560,128]{1,0:T(8,128)(2,1)S(1)}, bf16[560,128]{1,0:T(8,128)(2,1)S(1)}, u32[]{:S(2)}, u32[]{:S(2)}) collective-permute-start(bf16[560,128]{1,0:T(8,128)(2,1)S(1)} %copy-done.6), channel_id=1, source_target_pairs={{0,15},{2,13},{4,11},{6,9},{8,7},{10,5},{12,3},{14,1},{16,31},{18,... | collective-permute-start | bytes 430088 | tf_op jit(solution)/shard_map/ppermute | solution.py:746
  18.8 0.0 collective-permute-done.rest_0_
  18.8 1.3 %collective-permute-start.5 = (bf16[560,128]{1,0:T(8,128)(2,1)S(1)}, bf16[560,128]{1,0:T(8,128)(2,1)S(1)}, u32[]{:S(2)}, u32[]{:S(2)}) collective-permute-start(bf16[560,128]{1,0:T(8,128)(2,1)S(1)} %copy-done.5), channel_id=1, source_target_pairs={{0,11},{2,9},{4,15},{6,13},{8,3},{10,1},{12,7},{14,5},{16,27},{18,... | collective-permute-start | bytes 430088 | tf_op jit(solution)/shard_map/ppermute | solution.py:746
  20.1 2.7 %collective-permute-done.1.rest_1_ = bf16[560,128]{1,0:T(8,128)(2,1)S(1)} collective-permute-done((bf16[560,128]{1,0:T(8,128)(2,1)S(1)}, bf16[560,128]{1,0:T(8,128)(2,1)S(1)}, u32[]{:S(2)}, u32[]{:S(2)}) %collective-permute-start.1) | collective-permute-done | bytes 143392 | tf_op jit(solution)/shard_map/ppermute | solution.py:746
  22.8 1.3 %collective-permute-start.6 = (bf16[560,128]{1,0:T(8,128)(2,1)S(1)}, bf16[560,128]{1,0:T(8,128)(2,1)S(1)}, u32[]{:S(2)}, u32[]{:S(2)}) collective-permute-start(bf16[560,128]{1,0:T(8,128)(2,1)S(1)} %copy-done.4), channel_id=1, source_target_pairs={{0,13},{2,15},{4,9},{6,11},{8,5},{10,7},{12,1},{14,3},{16,29},{18,... | collective-permute-start | bytes 430088 | tf_op jit(solution)/shard_map/ppermute | solution.py:746
  24.1 8.0 %collective-permute-done.2.rest_2_ = bf16[560,128]{1,0:T(8,128)(2,1)S(1)} collective-permute-done((bf16[560,128]{1,0:T(8,128)(2,1)S(1)}, bf16[560,128]{1,0:T(8,128)(2,1)S(1)}, u32[]{:S(2)}, u32[]{:S(2)}) %collective-permute-start.2) | collective-permute-done | bytes 143392 | tf_op jit(solution)/shard_map/ppermute | solution.py:746
  32.1 0.0 copy-done.3
  32.1 1.3 %collective-permute-start.7 = (bf16[560,128]{1,0:T(8,128)(2,1)S(1)}, bf16[560,128]{1,0:T(8,128)(2,1)S(1)}, u32[]{:S(2)}, u32[]{:S(2)}) collective-permute-start(bf16[560,128]{1,0:T(8,128)(2,1)S(1)} %copy-done.3), channel_id=1, source_target_pairs={{0,7},{2,5},{4,3},{6,1},{8,15},{10,13},{12,11},{14,9},{16,23},{18,... | collective-permute-start | bytes 430088 | tf_op jit(solution)/shard_map/ppermute | solution.py:746
  33.4 0.0 copy-done.1
  33.5 0.1 copy.17
  33.6 0.2 reshape.35.taps_ref.first_taps_ref
  33.8 0.1 copy.16
  33.9 0.2 reshape.37.taps_ref.second_taps_ref
  34.1 14.0 %collective-permute-done.3.rest_3_ = bf16[560,128]{1,0:T(8,128)(2,1)S(1)} collective-permute-done((bf16[560,128]{1,0:T(8,128)(2,1)}, bf16[560,128]{1,0:T(8,128)(2,1)S(1)}, u32[]{:S(2)}, u32[]{:S(2)}) %collective-permute-start.3) | collective-permute-done | bytes 143392 | tf_op jit(solution)/shard_map/ppermute | solution.py:746
  48.1 0.0 collective-permute-done.4.rest_4_
  48.1 4.0 %collective-permute-done.5.rest_5_ = bf16[560,128]{1,0:T(8,128)(2,1)S(1)} collective-permute-done((bf16[560,128]{1,0:T(8,128)(2,1)S(1)}, bf16[560,128]{1,0:T(8,128)(2,1)S(1)}, u32[]{:S(2)}, u32[]{:S(2)}) %collective-permute-start.5) | collective-permute-done | bytes 143392 | tf_op jit(solution)/shard_map/ppermute | solution.py:746
  52.1 0.0 collective-permute-done.6.rest_6_
  52.1 0.0 collective-permute-done.7.rest_7_
  52.1 0.0 all-to-all-done
  52.1 0.1 broadcast_in_dim.12.gain_ref
  52.2 1.8 %gather_rows.1 = (f32[33,72,128]{2,1,0:T(8,128)S(1)}, bf16[3,80,128]{2,1,0:T(8,128)(2,1)S(1)}, bf16[3,80,128]{2,1,0:T(8,128)(2,1)S(1)}, bf16[80,128]{1,0:T(8,128)(2,1)S(1)}) custom-call(s32[1,2]{1,0:T(1,128)S(1)} %copy-done, f32[72,128]{1,0:T(8,128)S(1)} %broadcast_in_dim.12.gain_ref, bf16[4480,128]{1,0:T(8,128)(2,1)S(1)} %bitcast.24, ...), custom_call_target="tpu_custom_call" | custom-call | tf_op jit(solution)/shard_map/gather_rows/pallas_call | solution.py:300
  54.0 0.1 collective-permute-start.8
  54.1 0.5 collective-permute-start.9
  54.6 0.3 normalize_rows.1
  54.9 1.1 %channels_first.1 = bf16[2208,128]{1,0:T(8,128)(2,1)} custom-call(bf16[32,72,128]{2,1,0:T(8,128)(2,1)S(1)} %get-tuple-element.59.field.gridded), custom_call_target="tpu_custom_call" | custom-call | tf_op jit(solution)/shard_map/channels_first/pallas_call | solution.py:317
  56.0 1.2 %inner_convolution.1 = (bf16[32,80,128]{2,1,0:T(8,128)(2,1)S(1)}, f32[2,80,128]{2,1,0:T(8,128)S(1)}, f32[2,80,128]{2,1,0:T(8,128)S(1)}) custom-call(bf16[240,240]{1,0:T(8,128)(2,1)S(1)} %reshape.35.taps_ref.first_taps_ref, bf16[32,80,128]{2,1,0:T(8,128)(2,1)S(1)} %get-tuple-element.62.field), custom_call_target="tpu_custom_call" | custom-call | flops 471859200 | bytes 2097152 | tf_op jit(solution)/shard_map/inner_convolution/pallas_call | solution.py:382
  57.2 0.0 collective-permute-done.8.above
  57.2 0.6 collective-permute-done.9.below
  57.8 0.1 half_strip_packs.1
  57.8 0.9 %collective-permute-start.10 = (bf16[2,80,128]{2,1,0:T(8,128)(2,1)S(1)}, bf16[2,80,128]{2,1,0:T(8,128)(2,1)S(1)}, u32[]{:S(2)}, u32[]{:S(2)}) collective-permute-start(bf16[2,80,128]{2,1,0:T(8,128)(2,1)S(1)} %get-tuple-element.74), channel_id=1, source_target_pairs={{0,3},{1,4},{2,5},{3,6},{4,7},{5,8},{6,9},{7,10},{8,11},{9,12},{10... | collective-permute-start | bytes 122888 | tf_op jit(solution)/shard_map/ppermute | solution.py:729
  58.7 3.6 %collective-permute-start.11 = (bf16[2,80,128]{2,1,0:T(8,128)(2,1)S(1)}, bf16[2,80,128]{2,1,0:T(8,128)(2,1)S(1)}, u32[]{:S(2)}, u32[]{:S(2)}) collective-permute-start(bf16[2,80,128]{2,1,0:T(8,128)(2,1)S(1)} %get-tuple-element.75), channel_id=1, source_target_pairs={{0,13},{1,14},{2,15},{3,0},{4,1},{5,2},{6,3},{7,4},{8,5},{9,6},{10... | collective-permute-start | bytes 122888 | tf_op jit(solution)/shard_map/ppermute | solution.py:729
  62.3 0.8 %inner_second_convolution.1.base = f32[32,72,128]{2,1,0:T(8,128)S(1)} custom-call(bf16[240,240]{1,0:T(8,128)(2,1)S(1)} %reshape.37.taps_ref.second_taps_ref, bf16[32,80,128]{2,1,0:T(8,128)(2,1)S(1)} %get-tuple-element.71.hidden, bf16[32,72,128]{2,1,0:T(8,128)(2,1)S(1)} %get-tuple-element.59.field.gridded), custom_call_target="tpu_custom_call" | custom-call | flops 471859200 | bytes 2097152 | tf_op jit(solution)/shard_map/inner_second_convolution/pallas_call | solution.py:415
  63.1 1.0 %collective-permute-done.10.rest_0_ = bf16[2,80,128]{2,1,0:T(8,128)(2,1)S(1)} collective-permute-done((bf16[2,80,128]{2,1,0:T(8,128)(2,1)S(1)}, bf16[2,80,128]{2,1,0:T(8,128)(2,1)S(1)}, u32[]{:S(2)}, u32[]{:S(2)}) %collective-permute-start.10) | collective-permute-done | bytes 40992 | tf_op jit(solution)/shard_map/ppermute | solution.py:729
  64.1 0.0 collective-permute-done.11.rest_1_
  64.1 2.9 %convolutions.1 = bf16[69,32,128]{2,1,0:T(8,128)(2,1)} custom-call(bf16[240,240]{1,0:T(8,128)(2,1)S(1)} %reshape.35.taps_ref.first_taps_ref, bf16[240,240]{1,0:T(8,128)(2,1)S(1)} %reshape.37.taps_ref.second_taps_ref, bf16[32,80,128]{2,1,0:T(8,128)(2,1)S(1)} %get-tuple-element.62.field, f32[32,72,128]{2,1,0:T(8,128)S(1)} %inner_second_convolution.1.base, ...), custom_call_target="tpu_custom_call" | custom-call | tf_op jit(solution)/shard_map/convolutions/pallas_call | solution.py:706
  (16 shorter events, 0.1 us)
Async XLA Ops:
  5.6 6.6 %copy-start.9 = (bf16[560,128]{1,0:T(8,128)(2,1)S(1)}, bf16[560,128]{1,0:T(8,128)(2,1)}, u32[]{:S(2)}) copy-start(bf16[560,128]{1,0:T(8,128)(2,1)} %get-tuple-element.40) | copy-start | bytes 430084
  5.6 7.9 %copy-start.8 = (bf16[560,128]{1,0:T(8,128)(2,1)S(1)}, bf16[560,128]{1,0:T(8,128)(2,1)}, u32[]{:S(2)}) copy-start(bf16[560,128]{1,0:T(8,128)(2,1)} %get-tuple-element.41) | copy-start | bytes 430084
  5.6 9.2 %copy-start.7 = (bf16[560,128]{1,0:T(8,128)(2,1)S(1)}, bf16[560,128]{1,0:T(8,128)(2,1)}, u32[]{:S(2)}) copy-start(bf16[560,128]{1,0:T(8,128)(2,1)} %get-tuple-element.42) | copy-start | bytes 430084
  5.7 11.8 %copy-start.6 = (bf16[560,128]{1,0:T(8,128)(2,1)S(1)}, bf16[560,128]{1,0:T(8,128)(2,1)}, u32[]{:S(2)}) copy-start(bf16[560,128]{1,0:T(8,128)(2,1)} %get-tuple-element.44) | copy-start | bytes 430084
  5.7 13.2 %copy-start.5 = (bf16[560,128]{1,0:T(8,128)(2,1)S(1)}, bf16[560,128]{1,0:T(8,128)(2,1)}, u32[]{:S(2)}) copy-start(bf16[560,128]{1,0:T(8,128)(2,1)} %get-tuple-element.45) | copy-start | bytes 430084
  5.7 17.1 %copy-start.4 = (bf16[560,128]{1,0:T(8,128)(2,1)S(1)}, bf16[560,128]{1,0:T(8,128)(2,1)}, u32[]{:S(2)}) copy-start(bf16[560,128]{1,0:T(8,128)(2,1)} %get-tuple-element.46) | copy-start | bytes 430084
  5.7 26.4 %copy-start.3 = (bf16[560,128]{1,0:T(8,128)(2,1)S(1)}, bf16[560,128]{1,0:T(8,128)(2,1)}, u32[]{:S(2)}) copy-start(bf16[560,128]{1,0:T(8,128)(2,1)} %get-tuple-element.47) | copy-start | bytes 430084
  5.7 27.7 %copy-start.1 = (bf16[9,69,69]{2,1,0:T(8,128)(2,1)S(1)}, bf16[9,69,69]{2,1,0:T(8,128)(2,1)}, u32[]{:S(2)}) copy-start(bf16[9,69,69]{2,1,0:T(8,128)(2,1)} %param.14) | copy-start | bytes 257098
  5.7 28.0 %copy-start.2 = (bf16[9,69,69]{2,1,0:T(8,128)(2,1)S(1)}, bf16[9,69,69]{2,1,0:T(8,128)(2,1)}, u32[]{:S(2)}) copy-start(bf16[9,69,69]{2,1,0:T(8,128)(2,1)} %param.15) | copy-start | bytes 257098
  5.7 46.4 %all-to-all-start = ((bf16[8,560,128]{2,1,0:T(8,128)(2,1)}), bf16[8,560,128]{2,1,0:T(8,128)(2,1)S(1)}, u32[]{:S(2)}, u32[]{:S(2)}) async-start(bf16[8,560,128]{2,1,0:T(8,128)(2,1)} %bitcast.25), calls=%async_computation | async-start | bytes 2293760 | tf_op jit(solution)/shard_map/all_to_all | solution.py:748
  12.3 21.8 %copy-start.10 = (f32[69]{0:T(128)S(1)}, f32[69]{0:T(128)}, u32[]{:S(2)}) copy-start(f32[69]{0:T(128)} %param.13) | copy-start | bytes 832
  12.3 6.5 %collective-permute-start = (bf16[560,128]{1,0:T(8,128)(2,1)S(1)}, bf16[560,128]{1,0:T(8,128)(2,1)S(1)}, u32[]{:S(2)}, u32[]{:S(2)}) collective-permute-start(bf16[560,128]{1,0:T(8,128)(2,1)S(1)} %copy-done.9), channel_id=1, source_target_pairs={{0,1},{2,3},{4,5},{6,7},{8,9},{10,11},{12,13},{14,15},{16,17},{18,... | collective-permute-start | bytes 430088 | tf_op jit(solution)/shard_map/ppermute | solution.py:746
  13.6 38.6 %copy-start = (s32[1,2]{1,0:T(1,128)S(1)}, s32[1,2]{1,0:T(1,128)}, u32[]{:S(2)}) copy-start(s32[1,2]{1,0:T(1,128)} %flip_ref.1) | copy-start | bytes 28
  13.6 9.2 %collective-permute-start.1 = (bf16[560,128]{1,0:T(8,128)(2,1)S(1)}, bf16[560,128]{1,0:T(8,128)(2,1)S(1)}, u32[]{:S(2)}, u32[]{:S(2)}) collective-permute-start(bf16[560,128]{1,0:T(8,128)(2,1)S(1)} %copy-done.8), channel_id=1, source_target_pairs={{0,3},{2,1},{4,7},{6,5},{8,11},{10,9},{12,15},{14,13},{16,19},{18,... | collective-permute-start | bytes 430088 | tf_op jit(solution)/shard_map/ppermute | solution.py:746
  14.9 17.2 %collective-permute-start.2 = (bf16[560,128]{1,0:T(8,128)(2,1)S(1)}, bf16[560,128]{1,0:T(8,128)(2,1)S(1)}, u32[]{:S(2)}, u32[]{:S(2)}) collective-permute-start(bf16[560,128]{1,0:T(8,128)(2,1)S(1)} %copy-done.7), channel_id=1, source_target_pairs={{0,5},{2,7},{4,1},{6,3},{8,13},{10,15},{12,9},{14,11},{16,21},{18,... | collective-permute-start | bytes 430088 | tf_op jit(solution)/shard_map/ppermute | solution.py:746
  16.2 31.9 %collective-permute-start.3 = (bf16[560,128]{1,0:T(8,128)(2,1)}, bf16[560,128]{1,0:T(8,128)(2,1)S(1)}, u32[]{:S(2)}, u32[]{:S(2)}) collective-permute-start(bf16[560,128]{1,0:T(8,128)(2,1)} %get-tuple-element.43), channel_id=1, source_target_pairs={{0,9},{2,11},{4,13},{6,15},{8,1},{10,3},{12,5},{14,7},{16,25},{18,... | collective-permute-start | bytes 430088 | tf_op jit(solution)/shard_map/ppermute | solution.py:746
  17.5 30.6 %collective-permute-start.4 = (bf16[560,128]{1,0:T(8,128)(2,1)S(1)}, bf16[560,128]{1,0:T(8,128)(2,1)S(1)}, u32[]{:S(2)}, u32[]{:S(2)}) collective-permute-start(bf16[560,128]{1,0:T(8,128)(2,1)S(1)} %copy-done.6), channel_id=1, source_target_pairs={{0,15},{2,13},{4,11},{6,9},{8,7},{10,5},{12,3},{14,1},{16,31},{18,... | collective-permute-start | bytes 430088 | tf_op jit(solution)/shard_map/ppermute | solution.py:746
  18.8 33.3 %collective-permute-start.5 = (bf16[560,128]{1,0:T(8,128)(2,1)S(1)}, bf16[560,128]{1,0:T(8,128)(2,1)S(1)}, u32[]{:S(2)}, u32[]{:S(2)}) collective-permute-start(bf16[560,128]{1,0:T(8,128)(2,1)S(1)} %copy-done.5), channel_id=1, source_target_pairs={{0,11},{2,9},{4,15},{6,13},{8,3},{10,1},{12,7},{14,5},{16,27},{18,... | collective-permute-start | bytes 430088 | tf_op jit(solution)/shard_map/ppermute | solution.py:746
  22.8 29.3 %collective-permute-start.6 = (bf16[560,128]{1,0:T(8,128)(2,1)S(1)}, bf16[560,128]{1,0:T(8,128)(2,1)S(1)}, u32[]{:S(2)}, u32[]{:S(2)}) collective-permute-start(bf16[560,128]{1,0:T(8,128)(2,1)S(1)} %copy-done.4), channel_id=1, source_target_pairs={{0,13},{2,15},{4,9},{6,11},{8,5},{10,7},{12,1},{14,3},{16,29},{18,... | collective-permute-start | bytes 430088 | tf_op jit(solution)/shard_map/ppermute | solution.py:746
  32.1 20.0 %collective-permute-start.7 = (bf16[560,128]{1,0:T(8,128)(2,1)S(1)}, bf16[560,128]{1,0:T(8,128)(2,1)S(1)}, u32[]{:S(2)}, u32[]{:S(2)}) collective-permute-start(bf16[560,128]{1,0:T(8,128)(2,1)S(1)} %copy-done.3), channel_id=1, source_target_pairs={{0,7},{2,5},{4,3},{6,1},{8,15},{10,13},{12,11},{14,9},{16,23},{18,... | collective-permute-start | bytes 430088 | tf_op jit(solution)/shard_map/ppermute | solution.py:746
  54.0 3.2 %collective-permute-start.8 = (bf16[3,80,128]{2,1,0:T(8,128)(2,1)S(1)}, bf16[3,80,128]{2,1,0:T(8,128)(2,1)S(1)}, u32[]{:S(2)}, u32[]{:S(2)}) collective-permute-start(bf16[3,80,128]{2,1,0:T(8,128)(2,1)S(1)} %get-tuple-element.63), channel_id=1, source_target_pairs={{0,1},{1,2},{2,3},{3,4},{4,5},{5,6},{6,7},{7,8},{8,9},{9,10},{10,1... | collective-permute-start | bytes 184328 | tf_op jit(solution)/shard_map/ppermute | solution.py:729
  54.1 3.7 %collective-permute-start.9 = (bf16[3,80,128]{2,1,0:T(8,128)(2,1)S(1)}, bf16[3,80,128]{2,1,0:T(8,128)(2,1)S(1)}, u32[]{:S(2)}, u32[]{:S(2)}) collective-permute-start(bf16[3,80,128]{2,1,0:T(8,128)(2,1)S(1)} %get-tuple-element.64), channel_id=1, source_target_pairs={{0,15},{1,0},{2,1},{3,2},{4,3},{5,4},{6,5},{7,6},{8,7},{9,8},{10,9... | collective-permute-start | bytes 184328 | tf_op jit(solution)/shard_map/ppermute | solution.py:729
  57.8 6.3 %collective-permute-start.10 = (bf16[2,80,128]{2,1,0:T(8,128)(2,1)S(1)}, bf16[2,80,128]{2,1,0:T(8,128)(2,1)S(1)}, u32[]{:S(2)}, u32[]{:S(2)}) collective-permute-start(bf16[2,80,128]{2,1,0:T(8,128)(2,1)S(1)} %get-tuple-element.74), channel_id=1, source_target_pairs={{0,3},{1,4},{2,5},{3,6},{4,7},{5,8},{6,9},{7,10},{8,11},{9,12},{10... | collective-permute-start | bytes 122888 | tf_op jit(solution)/shard_map/ppermute | solution.py:729
  58.7 5.4 %collective-permute-start.11 = (bf16[2,80,128]{2,1,0:T(8,128)(2,1)S(1)}, bf16[2,80,128]{2,1,0:T(8,128)(2,1)S(1)}, u32[]{:S(2)}, u32[]{:S(2)}) collective-permute-start(bf16[2,80,128]{2,1,0:T(8,128)(2,1)S(1)} %get-tuple-element.75), channel_id=1, source_target_pairs={{0,13},{1,14},{2,15},{3,0},{4,1},{5,2},{6,3},{7,4},{8,5},{9,6},{10... | collective-permute-start | bytes 122888 | tf_op jit(solution)/shard_map/ppermute | solution.py:729
where the time goes:
time: 67.4 us; the launch traced here: 67.1 us
  waiting for transfers between devices  30.3 us (45%)
  starting transfers between devices  21.9 us (32%)
  Pallas kernels  13.2 us (20%)
  between operations  0.97 us (1%)
  local copies, waits for them, and re-layouts  0.71 us (1%)
    ppermute x8, waiting for transfers between devices, per_device(): nexts[across] = lax.ppermute(nexts[across], 'tile', pairs)  28.7 us
    ppermute x8, starting transfers between devices, per_device(): nexts[across] = lax.ppermute(nexts[across], 'tile', pairs)  10.3 us
    all_to_all x1, starting transfers between devices, per_device(): lax.all_to_all(same, 'tile', 0, 0, axis_index_groups=[[c * column_rows +...  6.53 us
    ppermute x4, starting transfers between devices, from_shift(): lax.ppermute(value, 'tile', [(i, (i - shift) % count) for i in range(coun...  5.05 us
    pallas_call x1, Pallas kernels, regrid(): pl.pallas_call(functools.partial(regrid_kernel, column_rows), in_specs=[h...  4.99 us
    pallas_call x1, Pallas kernels, convolutions(): pl.pallas_call(functools.partial(conv_kernel, column_rows), in_specs=[vme...  2.95 us
    pallas_call x1, Pallas kernels, gather_rows(): pl.pallas_call(functools.partial(gather_kernel, column_rows), in_specs=[s...  1.8 us
    ppermute x4, waiting for transfers between devices, from_shift(): lax.ppermute(value, 'tile', [(i, (i - shift) % count) for i in range(coun...  1.6 us
  transfers between devices with their start and end apart: 13, of which 6 were waited for; matrix products, arithmetic and copies ran while one was open for 1% of the time, Pallas kernels for 5%

commit v1 on v0

--- a/solution.py
+++ b/solution.py
@@ -744,7 +744,7 @@
             for p in range(column_rows - 1)
         ]
         nexts[across] = lax.ppermute(nexts[across], "tile", pairs)
-    nexts = [nexts[across] for across in (0, 1, 2, 4, 7, 5, 6, 3)]
+    nexts = [nexts[across] for across in (0, 1, 2, 4, 5, 6, 7, 3)]
     same = lax.all_to_all(
         same,
         "tile",

time: 67.4 us -> 66.8 us (level)
  waiting for transfers between devices: 30.3 us -> 29.3 us
    ppermute x8, waiting for transfers between devices: 28.7 us -> 27.1 us  [per_device(): nexts[across] = lax.ppermute(nexts[across], 'tile', pairs)]
  transfers between devices with their start and end apart: 13 -> 13, of which waited for: 6 -> 7; matrix products, arithmetic and copies ran while one was open for 1% -> 1% of each run, Pallas kernels for 5% -> 5%
where the time goes in v1:
time: 66.8 us; the launch traced here: 66 us
  waiting for transfers between devices  29.3 us (44%)
  starting transfers between devices  21.9 us (33%)
  Pallas kernels  13.2 us (20%)
  between operations  0.98 us (1%)
  local copies, waits for them, and re-layouts  0.71 us (1%)
    ppermute x8, waiting for transfers between devices, per_device(): nexts[across] = lax.ppermute(nexts[across], 'tile', pairs)  27.1 us
    ppermute x8, starting transfers between devices, per_device(): nexts[across] = lax.ppermute(nexts[across], 'tile', pairs)  10.3 us
    all_to_all x1, starting transfers between devices, per_device(): lax.all_to_all(same, 'tile', 0, 0, axis_index_groups=[[c * column_rows +...  6.53 us
    ppermute x4, starting transfers between devices, from_shift(): lax.ppermute(value, 'tile', [(i, (i - shift) % count) for i in range(coun...  5.05 us
    pallas_call x1, Pallas kernels, regrid(): pl.pallas_call(functools.partial(regrid_kernel, column_rows), in_specs=[h...  4.99 us
    pallas_call x1, Pallas kernels, convolutions(): pl.pallas_call(functools.partial(conv_kernel, column_rows), in_specs=[vme...  2.94 us
    ppermute x4, waiting for transfers between devices, from_shift(): lax.ppermute(value, 'tile', [(i, (i - shift) % count) for i in range(coun...  2.15 us
    pallas_call x1, Pallas kernels, gather_rows(): pl.pallas_call(functools.partial(gather_kernel, column_rows), in_specs=[s...  1.8 us
  transfers between devices with their start and end apart: 13, of which 7 were waited for; matrix products, arithmetic and copies ran while one was open for 1% of the time, Pallas kernels for 5%

profile of v1, /device:TPU:1, one launch (start us, length us, event | category | flops | bytes accessed | tf_op | source)
XLA Modules:
  0.0 66.0 jit_solution(7461612314358095567)
XLA Ops:
  0.6 5.0 %regrid.1 = (bf16[4480,128]{1,0:T(8,128)(2,1)}, bf16[560,128]{1,0:T(8,128)(2,1)}, bf16[560,128]{1,0:T(8,128)(2,1)}, bf16[560,128]{1,0:T(8,128)(2,1)}, bf16[560,1...) custom-call(s32[96]{0:T(128)} %target_hbm.1, ...), custom_call_target="tpu_custom_call" | custom-call | tf_op jit(solution)/shard_map/regrid/pallas_call | solution.py:181
  5.6 0.0 copy-start.9
  5.6 0.0 copy-start.8
  5.7 0.0 copy-start.7
  5.7 0.0 copy-start.1
  5.7 0.0 copy-start.2
  5.7 6.5 %all-to-all-start = ((bf16[8,560,128]{2,1,0:T(8,128)(2,1)}), bf16[8,560,128]{2,1,0:T(8,128)(2,1)S(1)}, u32[]{:S(2)}, u32[]{:S(2)}) async-start(bf16[8,560,128]{2,1,0:T(8,128)(2,1)} %bitcast.25), calls=%async_computation | async-start | bytes 2293760 | tf_op jit(solution)/shard_map/all_to_all | solution.py:748
  12.3 0.0 copy-done.9
  12.3 1.3 %collective-permute-start = (bf16[560,128]{1,0:T(8,128)(2,1)S(1)}, bf16[560,128]{1,0:T(8,128)(2,1)S(1)}, u32[]{:S(2)}, u32[]{:S(2)}) collective-permute-start(bf16[560,128]{1,0:T(8,128)(2,1)S(1)} %copy-done.9), channel_id=1, source_target_pairs={{0,1},{2,3},{4,5},{6,7},{8,9},{10,11},{12,13},{14,15},{16,17},{18,... | collective-permute-start | bytes 430088 | tf_op jit(solution)/shard_map/ppermute | solution.py:746
  13.6 0.0 copy-done.8
  13.6 0.0 copy-start
  13.6 1.3 %collective-permute-start.1 = (bf16[560,128]{1,0:T(8,128)(2,1)S(1)}, bf16[560,128]{1,0:T(8,128)(2,1)S(1)}, u32[]{:S(2)}, u32[]{:S(2)}) collective-permute-start(bf16[560,128]{1,0:T(8,128)(2,1)S(1)} %copy-done.8), channel_id=1, source_target_pairs={{0,3},{2,1},{4,7},{6,5},{8,11},{10,9},{12,15},{14,13},{16,19},{18,... | collective-permute-start | bytes 430088 | tf_op jit(solution)/shard_map/ppermute | solution.py:746
  14.9 1.3 %collective-permute-start.2 = (bf16[560,128]{1,0:T(8,128)(2,1)S(1)}, bf16[560,128]{1,0:T(8,128)(2,1)S(1)}, u32[]{:S(2)}, u32[]{:S(2)}) collective-permute-start(bf16[560,128]{1,0:T(8,128)(2,1)S(1)} %copy-done.7), channel_id=1, source_target_pairs={{0,5},{2,7},{4,1},{6,3},{8,13},{10,15},{12,9},{14,11},{16,21},{18,... | collective-permute-start | bytes 430088 | tf_op jit(solution)/shard_map/ppermute | solution.py:746
  16.2 1.3 %collective-permute-start.3 = (bf16[560,128]{1,0:T(8,128)(2,1)}, bf16[560,128]{1,0:T(8,128)(2,1)S(1)}, u32[]{:S(2)}, u32[]{:S(2)}) collective-permute-start(bf16[560,128]{1,0:T(8,128)(2,1)} %get-tuple-element.43), channel_id=1, source_target_pairs={{0,9},{2,11},{4,13},{6,15},{8,1},{10,3},{12,5},{14,7},{16,25},{18,... | collective-permute-start | bytes 430088 | tf_op jit(solution)/shard_map/ppermute | solution.py:746
  17.5 1.3 %collective-permute-start.4 = (bf16[560,128]{1,0:T(8,128)(2,1)S(1)}, bf16[560,128]{1,0:T(8,128)(2,1)S(1)}, u32[]{:S(2)}, u32[]{:S(2)}) collective-permute-start(bf16[560,128]{1,0:T(8,128)(2,1)S(1)} %copy-done.6), channel_id=1, source_target_pairs={{0,11},{2,9},{4,15},{6,13},{8,3},{10,1},{12,7},{14,5},{16,27},{18,... | collective-permute-start | bytes 430088 | tf_op jit(solution)/shard_map/ppermute | solution.py:746
  18.8 0.0 collective-permute-done.rest_0_
  18.8 1.3 %collective-permute-start.5 = (bf16[560,128]{1,0:T(8,128)(2,1)S(1)}, bf16[560,128]{1,0:T(8,128)(2,1)S(1)}, u32[]{:S(2)}, u32[]{:S(2)}) collective-permute-start(bf16[560,128]{1,0:T(8,128)(2,1)S(1)} %copy-done.5), channel_id=1, source_target_pairs={{0,13},{2,15},{4,9},{6,11},{8,5},{10,7},{12,1},{14,3},{16,29},{18,... | collective-permute-start | bytes 430088 | tf_op jit(solution)/shard_map/ppermute | solution.py:746
  20.1 2.7 %collective-permute-done.1.rest_1_ = bf16[560,128]{1,0:T(8,128)(2,1)S(1)} collective-permute-done((bf16[560,128]{1,0:T(8,128)(2,1)S(1)}, bf16[560,128]{1,0:T(8,128)(2,1)S(1)}, u32[]{:S(2)}, u32[]{:S(2)}) %collective-permute-start.1) | collective-permute-done | bytes 143392 | tf_op jit(solution)/shard_map/ppermute | solution.py:746
  22.8 1.3 %collective-permute-start.6 = (bf16[560,128]{1,0:T(8,128)(2,1)S(1)}, bf16[560,128]{1,0:T(8,128)(2,1)S(1)}, u32[]{:S(2)}, u32[]{:S(2)}) collective-permute-start(bf16[560,128]{1,0:T(8,128)(2,1)S(1)} %copy-done.4), channel_id=1, source_target_pairs={{0,15},{2,13},{4,11},{6,9},{8,7},{10,5},{12,3},{14,1},{16,31},{18,... | collective-permute-start | bytes 430088 | tf_op jit(solution)/shard_map/ppermute | solution.py:746
  24.1 8.0 %collective-permute-done.2.rest_2_ = bf16[560,128]{1,0:T(8,128)(2,1)S(1)} collective-permute-done((bf16[560,128]{1,0:T(8,128)(2,1)S(1)}, bf16[560,128]{1,0:T(8,128)(2,1)S(1)}, u32[]{:S(2)}, u32[]{:S(2)}) %collective-permute-start.2) | collective-permute-done | bytes 143392 | tf_op jit(solution)/shard_map/ppermute | solution.py:746
  32.1 1.3 %collective-permute-start.7 = (bf16[560,128]{1,0:T(8,128)(2,1)S(1)}, bf16[560,128]{1,0:T(8,128)(2,1)S(1)}, u32[]{:S(2)}, u32[]{:S(2)}) collective-permute-start(bf16[560,128]{1,0:T(8,128)(2,1)S(1)} %copy-done.3), channel_id=1, source_target_pairs={{0,7},{2,5},{4,3},{6,1},{8,15},{10,13},{12,11},{14,9},{16,23},{18,... | collective-permute-start | bytes 430088 | tf_op jit(solution)/shard_map/ppermute | solution.py:746
  33.5 0.1 copy.17
  33.6 0.2 reshape.35.taps_ref.first_taps_ref
  33.8 0.1 copy.16
  33.9 0.2 reshape.37.taps_ref.second_taps_ref
  34.1 14.0 %collective-permute-done.3.rest_3_ = bf16[560,128]{1,0:T(8,128)(2,1)S(1)} collective-permute-done((bf16[560,128]{1,0:T(8,128)(2,1)}, bf16[560,128]{1,0:T(8,128)(2,1)S(1)}, u32[]{:S(2)}, u32[]{:S(2)}) %collective-permute-start.3) | collective-permute-done | bytes 143392 | tf_op jit(solution)/shard_map/ppermute | solution.py:746
  48.1 2.4 %collective-permute-done.4.rest_4_ = bf16[560,128]{1,0:T(8,128)(2,1)S(1)} collective-permute-done((bf16[560,128]{1,0:T(8,128)(2,1)S(1)}, bf16[560,128]{1,0:T(8,128)(2,1)S(1)}, u32[]{:S(2)}, u32[]{:S(2)}) %collective-permute-start.4) | collective-permute-done | bytes 143392 | tf_op jit(solution)/shard_map/ppermute | solution.py:746
  50.5 0.0 collective-permute-done.5.rest_5_
  50.5 0.0 collective-permute-done.6.rest_6_
  50.5 0.0 collective-permute-done.7.rest_7_
  50.5 0.0 all-to-all-done
  50.5 0.1 broadcast_in_dim.12.gain_ref
  50.6 0.0 copy-done
  50.6 1.8 %gather_rows.1 = (f32[33,72,128]{2,1,0:T(8,128)S(1)}, bf16[3,80,128]{2,1,0:T(8,128)(2,1)S(1)}, bf16[3,80,128]{2,1,0:T(8,128)(2,1)S(1)}, bf16[80,128]{1,0:T(8,128)(2,1)S(1)}) custom-call(s32[1,2]{1,0:T(1,128)S(1)} %copy-done, f32[72,128]{1,0:T(8,128)S(1)} %broadcast_in_dim.12.gain_ref, bf16[4480,128]{1,0:T(8,128)(2,1)S(1)} %bitcast.24, ...), custom_call_target="tpu_custom_call" | custom-call | tf_op jit(solution)/shard_map/gather_rows/pallas_call | solution.py:300
  52.4 0.1 collective-permute-start.8
  52.5 0.5 collective-permute-start.9
  53.0 0.3 normalize_rows.1
  53.3 1.1 %channels_first.1 = bf16[2208,128]{1,0:T(8,128)(2,1)} custom-call(bf16[32,72,128]{2,1,0:T(8,128)(2,1)S(1)} %get-tuple-element.59.field.gridded), custom_call_target="tpu_custom_call" | custom-call | tf_op jit(solution)/shard_map/channels_first/pallas_call | solution.py:317
  54.4 1.2 %inner_convolution.1 = (bf16[32,80,128]{2,1,0:T(8,128)(2,1)S(1)}, f32[2,80,128]{2,1,0:T(8,128)S(1)}, f32[2,80,128]{2,1,0:T(8,128)S(1)}) custom-call(bf16[240,240]{1,0:T(8,128)(2,1)S(1)} %reshape.35.taps_ref.first_taps_ref, bf16[32,80,128]{2,1,0:T(8,128)(2,1)S(1)} %get-tuple-element.62.field), custom_call_target="tpu_custom_call" | custom-call | flops 471859200 | bytes 2097152 | tf_op jit(solution)/shard_map/inner_convolution/pallas_call | solution.py:382
  55.6 0.0 collective-permute-done.8.above
  55.6 0.6 collective-permute-done.9.below
  56.2 0.1 half_strip_packs.1
  56.3 2.7 %collective-permute-start.10 = (bf16[2,80,128]{2,1,0:T(8,128)(2,1)S(1)}, bf16[2,80,128]{2,1,0:T(8,128)(2,1)S(1)}, u32[]{:S(2)}, u32[]{:S(2)}) collective-permute-start(bf16[2,80,128]{2,1,0:T(8,128)(2,1)S(1)} %get-tuple-element.74), channel_id=1, source_target_pairs={{0,3},{1,4},{2,5},{3,6},{4,7},{5,8},{6,9},{7,10},{8,11},{9,12},{10... | collective-permute-start | bytes 122888 | tf_op jit(solution)/shard_map/ppermute | solution.py:729
  59.0 1.8 %collective-permute-start.11 = (bf16[2,80,128]{2,1,0:T(8,128)(2,1)S(1)}, bf16[2,80,128]{2,1,0:T(8,128)(2,1)S(1)}, u32[]{:S(2)}, u32[]{:S(2)}) collective-permute-start(bf16[2,80,128]{2,1,0:T(8,128)(2,1)S(1)} %get-tuple-element.75), channel_id=1, source_target_pairs={{0,13},{1,14},{2,15},{3,0},{4,1},{5,2},{6,3},{7,4},{8,5},{9,6},{10... | collective-permute-start | bytes 122888 | tf_op jit(solution)/shard_map/ppermute | solution.py:729
  60.8 0.8 %inner_second_convolution.1.base = f32[32,72,128]{2,1,0:T(8,128)S(1)} custom-call(bf16[240,240]{1,0:T(8,128)(2,1)S(1)} %reshape.37.taps_ref.second_taps_ref, bf16[32,80,128]{2,1,0:T(8,128)(2,1)S(1)} %get-tuple-element.71.hidden, bf16[32,72,128]{2,1,0:T(8,128)(2,1)S(1)} %get-tuple-element.59.field.gridded), custom_call_target="tpu_custom_call" | custom-call | flops 471859200 | bytes 2097152 | tf_op jit(solution)/shard_map/inner_second_convolution/pallas_call | solution.py:415
  61.5 0.9 %collective-permute-done.10.rest_0_ = bf16[2,80,128]{2,1,0:T(8,128)(2,1)S(1)} collective-permute-done((bf16[2,80,128]{2,1,0:T(8,128)(2,1)S(1)}, bf16[2,80,128]{2,1,0:T(8,128)(2,1)S(1)}, u32[]{:S(2)}, u32[]{:S(2)}) %collective-permute-start.10) | collective-permute-done | bytes 40992 | tf_op jit(solution)/shard_map/ppermute | solution.py:729
  62.5 0.6 collective-permute-done.11.rest_1_
  63.1 2.9 %convolutions.1 = bf16[69,32,128]{2,1,0:T(8,128)(2,1)} custom-call(bf16[240,240]{1,0:T(8,128)(2,1)S(1)} %reshape.35.taps_ref.first_taps_ref, bf16[240,240]{1,0:T(8,128)(2,1)S(1)} %reshape.37.taps_ref.second_taps_ref, bf16[32,80,128]{2,1,0:T(8,128)(2,1)S(1)} %get-tuple-element.62.field, f32[32,72,128]{2,1,0:T(8,128)S(1)} %inner_second_convolution.1.base, ...), custom_call_target="tpu_custom_call" | custom-call | tf_op jit(solution)/shard_map/convolutions/pallas_call | solution.py:706
  (16 shorter events, 0.1 us)
Async XLA Ops:
  5.6 6.6 %copy-start.9 = (bf16[560,128]{1,0:T(8,128)(2,1)S(1)}, bf16[560,128]{1,0:T(8,128)(2,1)}, u32[]{:S(2)}) copy-start(bf16[560,128]{1,0:T(8,128)(2,1)} %get-tuple-element.40) | copy-start | bytes 430084
  5.6 7.9 %copy-start.8 = (bf16[560,128]{1,0:T(8,128)(2,1)S(1)}, bf16[560,128]{1,0:T(8,128)(2,1)}, u32[]{:S(2)}) copy-start(bf16[560,128]{1,0:T(8,128)(2,1)} %get-tuple-element.41) | copy-start | bytes 430084
  5.7 9.2 %copy-start.7 = (bf16[560,128]{1,0:T(8,128)(2,1)S(1)}, bf16[560,128]{1,0:T(8,128)(2,1)}, u32[]{:S(2)}) copy-start(bf16[560,128]{1,0:T(8,128)(2,1)} %get-tuple-element.42) | copy-start | bytes 430084
  5.7 11.8 %copy-start.6 = (bf16[560,128]{1,0:T(8,128)(2,1)S(1)}, bf16[560,128]{1,0:T(8,128)(2,1)}, u32[]{:S(2)}) copy-start(bf16[560,128]{1,0:T(8,128)(2,1)} %get-tuple-element.44) | copy-start | bytes 430084
  5.7 13.2 %copy-start.5 = (bf16[560,128]{1,0:T(8,128)(2,1)S(1)}, bf16[560,128]{1,0:T(8,128)(2,1)}, u32[]{:S(2)}) copy-start(bf16[560,128]{1,0:T(8,128)(2,1)} %get-tuple-element.45) | copy-start | bytes 430084
  5.7 17.1 %copy-start.4 = (bf16[560,128]{1,0:T(8,128)(2,1)S(1)}, bf16[560,128]{1,0:T(8,128)(2,1)}, u32[]{:S(2)}) copy-start(bf16[560,128]{1,0:T(8,128)(2,1)} %get-tuple-element.46) | copy-start | bytes 430084
  5.7 26.4 %copy-start.3 = (bf16[560,128]{1,0:T(8,128)(2,1)S(1)}, bf16[560,128]{1,0:T(8,128)(2,1)}, u32[]{:S(2)}) copy-start(bf16[560,128]{1,0:T(8,128)(2,1)} %get-tuple-element.47) | copy-start | bytes 430084
  5.7 27.7 %copy-start.1 = (bf16[9,69,69]{2,1,0:T(8,128)(2,1)S(1)}, bf16[9,69,69]{2,1,0:T(8,128)(2,1)}, u32[]{:S(2)}) copy-start(bf16[9,69,69]{2,1,0:T(8,128)(2,1)} %param.14) | copy-start | bytes 257098
  5.7 28.0 %copy-start.2 = (bf16[9,69,69]{2,1,0:T(8,128)(2,1)S(1)}, bf16[9,69,69]{2,1,0:T(8,128)(2,1)}, u32[]{:S(2)}) copy-start(bf16[9,69,69]{2,1,0:T(8,128)(2,1)} %param.15) | copy-start | bytes 257098
  5.7 44.8 %all-to-all-start = ((bf16[8,560,128]{2,1,0:T(8,128)(2,1)}), bf16[8,560,128]{2,1,0:T(8,128)(2,1)S(1)}, u32[]{:S(2)}, u32[]{:S(2)}) async-start(bf16[8,560,128]{2,1,0:T(8,128)(2,1)} %bitcast.25), calls=%async_computation | async-start | bytes 2293760 | tf_op jit(solution)/shard_map/all_to_all | solution.py:748
  12.3 21.8 %copy-start.10 = (f32[69]{0:T(128)S(1)}, f32[69]{0:T(128)}, u32[]{:S(2)}) copy-start(f32[69]{0:T(128)} %param.13) | copy-start | bytes 832
  12.3 6.5 %collective-permute-start = (bf16[560,128]{1,0:T(8,128)(2,1)S(1)}, bf16[560,128]{1,0:T(8,128)(2,1)S(1)}, u32[]{:S(2)}, u32[]{:S(2)}) collective-permute-start(bf16[560,128]{1,0:T(8,128)(2,1)S(1)} %copy-done.9), channel_id=1, source_target_pairs={{0,1},{2,3},{4,5},{6,7},{8,9},{10,11},{12,13},{14,15},{16,17},{18,... | collective-permute-start | bytes 430088 | tf_op jit(solution)/shard_map/ppermute | solution.py:746
  13.6 37.0 %copy-start = (s32[1,2]{1,0:T(1,128)S(1)}, s32[1,2]{1,0:T(1,128)}, u32[]{:S(2)}) copy-start(s32[1,2]{1,0:T(1,128)} %flip_ref.1) | copy-start | bytes 28
  13.6 9.2 %collective-permute-start.1 = (bf16[560,128]{1,0:T(8,128)(2,1)S(1)}, bf16[560,128]{1,0:T(8,128)(2,1)S(1)}, u32[]{:S(2)}, u32[]{:S(2)}) collective-permute-start(bf16[560,128]{1,0:T(8,128)(2,1)S(1)} %copy-done.8), channel_id=1, source_target_pairs={{0,3},{2,1},{4,7},{6,5},{8,11},{10,9},{12,15},{14,13},{16,19},{18,... | collective-permute-start | bytes 430088 | tf_op jit(solution)/shard_map/ppermute | solution.py:746
  14.9 17.2 %collective-permute-start.2 = (bf16[560,128]{1,0:T(8,128)(2,1)S(1)}, bf16[560,128]{1,0:T(8,128)(2,1)S(1)}, u32[]{:S(2)}, u32[]{:S(2)}) collective-permute-start(bf16[560,128]{1,0:T(8,128)(2,1)S(1)} %copy-done.7), channel_id=1, source_target_pairs={{0,5},{2,7},{4,1},{6,3},{8,13},{10,15},{12,9},{14,11},{16,21},{18,... | collective-permute-start | bytes 430088 | tf_op jit(solution)/shard_map/ppermute | solution.py:746
  16.2 31.9 %collective-permute-start.3 = (bf16[560,128]{1,0:T(8,128)(2,1)}, bf16[560,128]{1,0:T(8,128)(2,1)S(1)}, u32[]{:S(2)}, u32[]{:S(2)}) collective-permute-start(bf16[560,128]{1,0:T(8,128)(2,1)} %get-tuple-element.43), channel_id=1, source_target_pairs={{0,9},{2,11},{4,13},{6,15},{8,1},{10,3},{12,5},{14,7},{16,25},{18,... | collective-permute-start | bytes 430088 | tf_op jit(solution)/shard_map/ppermute | solution.py:746
  17.5 33.0 %collective-permute-start.4 = (bf16[560,128]{1,0:T(8,128)(2,1)S(1)}, bf16[560,128]{1,0:T(8,128)(2,1)S(1)}, u32[]{:S(2)}, u32[]{:S(2)}) collective-permute-start(bf16[560,128]{1,0:T(8,128)(2,1)S(1)} %copy-done.6), channel_id=1, source_target_pairs={{0,11},{2,9},{4,15},{6,13},{8,3},{10,1},{12,7},{14,5},{16,27},{18,... | collective-permute-start | bytes 430088 | tf_op jit(solution)/shard_map/ppermute | solution.py:746
  18.8 31.7 %collective-permute-start.5 = (bf16[560,128]{1,0:T(8,128)(2,1)S(1)}, bf16[560,128]{1,0:T(8,128)(2,1)S(1)}, u32[]{:S(2)}, u32[]{:S(2)}) collective-permute-start(bf16[560,128]{1,0:T(8,128)(2,1)S(1)} %copy-done.5), channel_id=1, source_target_pairs={{0,13},{2,15},{4,9},{6,11},{8,5},{10,7},{12,1},{14,3},{16,29},{18,... | collective-permute-start | bytes 430088 | tf_op jit(solution)/shard_map/ppermute | solution.py:746
  22.8 27.7 %collective-permute-start.6 = (bf16[560,128]{1,0:T(8,128)(2,1)S(1)}, bf16[560,128]{1,0:T(8,128)(2,1)S(1)}, u32[]{:S(2)}, u32[]{:S(2)}) collective-permute-start(bf16[560,128]{1,0:T(8,128)(2,1)S(1)} %copy-done.4), channel_id=1, source_target_pairs={{0,15},{2,13},{4,11},{6,9},{8,7},{10,5},{12,3},{14,1},{16,31},{18,... | collective-permute-start | bytes 430088 | tf_op jit(solution)/shard_map/ppermute | solution.py:746
  32.1 18.4 %collective-permute-start.7 = (bf16[560,128]{1,0:T(8,128)(2,1)S(1)}, bf16[560,128]{1,0:T(8,128)(2,1)S(1)}, u32[]{:S(2)}, u32[]{:S(2)}) collective-permute-start(bf16[560,128]{1,0:T(8,128)(2,1)S(1)} %copy-done.3), channel_id=1, source_target_pairs={{0,7},{2,5},{4,3},{6,1},{8,15},{10,13},{12,11},{14,9},{16,23},{18,... | collective-permute-start | bytes 430088 | tf_op jit(solution)/shard_map/ppermute | solution.py:746
  52.4 3.2 %collective-permute-start.8 = (bf16[3,80,128]{2,1,0:T(8,128)(2,1)S(1)}, bf16[3,80,128]{2,1,0:T(8,128)(2,1)S(1)}, u32[]{:S(2)}, u32[]{:S(2)}) collective-permute-start(bf16[3,80,128]{2,1,0:T(8,128)(2,1)S(1)} %get-tuple-element.63), channel_id=1, source_target_pairs={{0,1},{1,2},{2,3},{3,4},{4,5},{5,6},{6,7},{7,8},{8,9},{9,10},{10,1... | collective-permute-start | bytes 184328 | tf_op jit(solution)/shard_map/ppermute | solution.py:729
  52.5 3.7 %collective-permute-start.9 = (bf16[3,80,128]{2,1,0:T(8,128)(2,1)S(1)}, bf16[3,80,128]{2,1,0:T(8,128)(2,1)S(1)}, u32[]{:S(2)}, u32[]{:S(2)}) collective-permute-start(bf16[3,80,128]{2,1,0:T(8,128)(2,1)S(1)} %get-tuple-element.64), channel_id=1, source_target_pairs={{0,15},{1,0},{2,1},{3,2},{4,3},{5,4},{6,5},{7,6},{8,7},{9,8},{10,9... | collective-permute-start | bytes 184328 | tf_op jit(solution)/shard_map/ppermute | solution.py:729
  56.3 6.2 %collective-permute-start.10 = (bf16[2,80,128]{2,1,0:T(8,128)(2,1)S(1)}, bf16[2,80,128]{2,1,0:T(8,128)(2,1)S(1)}, u32[]{:S(2)}, u32[]{:S(2)}) collective-permute-start(bf16[2,80,128]{2,1,0:T(8,128)(2,1)S(1)} %get-tuple-element.74), channel_id=1, source_target_pairs={{0,3},{1,4},{2,5},{3,6},{4,7},{5,8},{6,9},{7,10},{8,11},{9,12},{10... | collective-permute-start | bytes 122888 | tf_op jit(solution)/shard_map/ppermute | solution.py:729
  59.0 4.1 %collective-permute-start.11 = (bf16[2,80,128]{2,1,0:T(8,128)(2,1)S(1)}, bf16[2,80,128]{2,1,0:T(8,128)(2,1)S(1)}, u32[]{:S(2)}, u32[]{:S(2)}) collective-permute-start(bf16[2,80,128]{2,1,0:T(8,128)(2,1)S(1)} %get-tuple-element.75), channel_id=1, source_target_pairs={{0,13},{1,14},{2,15},{3,0},{4,1},{5,2},{6,3},{7,4},{8,5},{9,6},{10... | collective-permute-start | bytes 122888 | tf_op jit(solution)/shard_map/ppermute | solution.py:729
